TPU v7x, 256 devices: a whole 4x4x8 slice. The times are simulated.
256 devices in a mesh: grp: 4 (over z_lo, core), dev: 64 (over y, z_hi, x).
Axes of the slice: x: 4, y: 4, z: 8 (z_hi: 4, z_lo: 2; z = z_hi * 2 + z_lo), core: 2. Of those that a mesh axis runs over, the one named last changes fastest.
Arguments:
- gradient: bfloat16 [64, 512, 2048], P('grp', 'dev'), may hold values from -400 to 400
- momentum: float32 [256, 512, 512], P(('grp', 'dev')), may hold values from -8 to 8
- master_weight: float32 [256, 512, 512], P(('grp', 'dev')), may hold values from -0.12 to 0.12
- owned_matrix: int32 [4, 16], replicated, may hold values from 0 to 15, each once within a row
- rollout_matrix: int32 [4, 64], P('grp'), may hold values from 0 to 63, each once within a row
Outputs:
- new_momentum: float32 [256, 512, 512], P(('grp', 'dev'))
- update: float32 [256, 512, 512], P(('grp', 'dev'))
- new_master: float32 [256, 512, 512], P(('grp', 'dev'))
- rollout_weight: bfloat16 [256, 512, 2048], P(('grp', 'dev'))
Inputs may be any that keep to these rules, and one draw needn't show every extreme that they name: Each row of owned_matrix lists every number 0 to 15 once. Each row of rollout_matrix lists every matrix 0 to 63 once.
All inputs are finite; a program needn't handle non-finite values.
Results may differ from a plain program's by a relative error of at most 0.001.
Values may be sent and summed in bfloat16 or wider, within the bound.
A program may use at most 64 MiB of HBM per device.

v0:
```python
import math

import jax
import jax.numpy as jnp
from jax import lax
from jax.experimental import pallas as pl
from jax.experimental.pallas import tpu as pltpu
from jax.sharding import PartitionSpec as P

MESH = pl.DeviceIdType.MESH
F32 = jnp.float32
BF16 = jnp.bfloat16

ITERS = 5
momentum_decay = 0.95
learn_rate = 0.02
weight_decay = 0.1
first_coeff = 3.4445
second_coeff = -4.775
third_coeff = 2.0315
norm_epsilon = 1e-07

N = 512
HALF = 256
QUADS = 16
DEVS = 64
CHUNKS = 8
DEPTH = 16
TILES = [(i, j) for i in range(4) for j in range(i, 4)]
PIECE = len(TILES) * 128 // 4


def split2(value):
    high = value.astype(BF16)
    return high, (value - high.astype(F32)).astype(BF16)


def split3(value):
    high = value.astype(BF16)
    rest = value - high.astype(F32)
    mid = rest.astype(BF16)
    return high, mid, (rest - mid.astype(F32)).astype(BF16)


def dot(left, right):
    return jnp.dot(left, right, preferred_element_type=F32)


def dot_t(left, right):
    return lax.dot_general(left, right, (((1,), (1,)), ((), ())), preferred_element_type=F32)


def terms(count):
    pairs = [(i, j) for i in range(count) for j in range(count) if i + j < count]
    return sorted(pairs, key=lambda pair: -sum(pair))


SCHEDULE = [
    (int(step[0]), int(step[1]))
    for step in (
        "01 11 31 21 41 12 02 32 51 13 22 03 42 14 33 61 04 23 10 34 52 71 00 43 24 30 62 53 44 72"
        " 20 63 54 40 73 64 50 74 60 70"
    ).split(" ")
]


def blocks_of(unit):
    return unit // 5, slice(unit % 5 * 64, (unit % 5 + 1) * 64)


def kernel(
    owned, wanted, grad_in, mom_in, master_in,
    mom_out, update_out, master_out, rollout_out,
    grad, mom, master, update,
    outbox, inbox, partial, others, full,
    a_ref, b_ref, t_ref, x_ref, p0, p1, p2, q0, q1, q2,
    rounded, chosen, names, table_v, table,
    in_sem, out_sem, names_send, names_recv, table_sem,
    send_sem, recv_sem, rs_send, rs_recv, ag_send, ag_recv,
    s1_send, s1_recv, up_send, up_recv, down_send, down_recv, s3_send, s3_recv, own_sem,
    *held,
):
    grp, dev = lax.axis_index("grp"), lax.axis_index("dev")
    x, z_hi, y = lax.rem(dev, 4), lax.rem(lax.div(dev, 4), 4), lax.div(dev, 16)
    z_lo, core = lax.div(grp, 2), lax.rem(grp, 2)
    z = z_hi * 2 + z_lo
    mine = y * 2 + core
    slot = z * 8 + mine

    def device(x, y, z, core):
        return (lax.rem(z, 2) * 2 + core, (y * 4 + lax.div(z, 2)) * 4 + x)

    def in_plane(index):
        across, along_y = lax.rem(lax.div(index, 2), 4), lax.div(index, 8)
        return (z_lo * 2 + lax.rem(index, 2), (along_y * 4 + z_hi) * 4 + across)

    here = (y * 4 + x) * 2 + core
    above, below = device(x, y, lax.rem(z + 1, 8), core), device(x, y, lax.rem(z + 7, 8), core)
    twin = (z_lo * 2 + 1 - core, dev)

    def remote(src, dst, sends, recvs, to):
        return pltpu.make_async_remote_copy(
            src_ref=src, dst_ref=dst, send_sem=sends, recv_sem=recvs, device_id=to, device_id_type=MESH
        )

    loads = [
        pltpu.make_async_copy(src, dst, in_sem.at[index])
        for index, (src, dst) in enumerate(
            ((grad_in, grad), (mom_in, mom), (master_in, master))
        )
    ]
    for copy in loads:
        copy.start()

    barrier = pltpu.get_barrier_semaphore()

    def greet(to):
        pl.semaphore_signal(barrier, inc=1, device_id=to, device_id_type=MESH)

    def greet_group(step, carry):
        greet((grp, lax.rem(dev + step, DEVS)))
        return carry

    def greet_plane(step, carry):
        greet((z_lo * 2 + 1 - core, in_plane(2 * step)[1]))
        return carry

    lax.fori_loop(1, DEVS, greet_group, 0)
    lax.fori_loop(0, 16, greet_plane, 0)
    greet(above)
    greet(below)

    names[0] = jnp.zeros((8, 128), jnp.int32)
    names[0, 0:1, 0:DEVS] = wanted[...]
    loads[0].wait()

    def fill(q, carry):
        rows = grad[owned[grp, q]].astype(F32)
        for c in range(4):
            left = rows[:, c * N : c * N + HALF]
            right = rows[:, c * N + HALF : (c + 1) * N]
            outbox[q * 4 + c] = jnp.concatenate([left, right], axis=0).astype(BF16)
        return carry

    lax.fori_loop(0, QUADS, fill, 0)
    pl.semaphore_wait(barrier, DEVS - 1 + 18)

    def send(step, carry):
        to = lax.rem(dev + step, DEVS)
        remote(outbox.at[to], inbox.at[dev], send_sem, recv_sem, (grp, to)).start()
        return carry

    lax.fori_loop(1, DEVS, send, 0)
    tell = remote(names.at[0], names.at[1], names_send, names_recv, twin)
    tell.start()
    inbox[dev] = outbox[dev]

    tell.wait_recv()
    found = [jnp.zeros((8, 128), jnp.int32), jnp.zeros((8, 128), jnp.int32)]
    own_names, twin_names = names[0], names[1]
    for group in range(4):
        for quad in range(QUADS):
            identity = group * QUADS + owned[group, quad]
            at = ((quad % 4) * 2 + group // 2) * 8 + (quad // 4) * 2 + group % 2
            found[0] = jnp.where(own_names == identity, at, found[0])
            found[1] = jnp.where(twin_names == identity, at, found[1])
    table_v[core] = found[0]
    table_v[1 - core] = found[1]
    lookup = pltpu.make_async_copy(table_v, table, table_sem)
    lookup.start()

    loads[1].wait()
    rest = pl.ds(0, DEVS - 1)
    everything = remote(
        outbox.at[rest], inbox.at[rest], send_sem, recv_sem, (grp, lax.rem(dev + 1, DEVS))
    )
    everything.wait_recv()

    lefts, rights = (p0, p1, p2), (q0, q1, q2)
    for r in range(4):
        got = inbox[pl.ds(r * 16, 16)].astype(F32)
        slab = jnp.concatenate(
            [got[:, :8, :].reshape(128, HALF), got[:, 8:, :].reshape(128, HALF)], axis=1
        )
        rows = slice(r * 128, (r + 1) * 128)
        moment = momentum_decay * mom[rows, :] + slab
        mom[rows, :] = moment
        nesterov = slab + momentum_decay * moment
        x_ref[rows, :] = nesterov
        for left, part in zip(lefts, split3(nesterov)):
            left[rows, :] = part
    stores = [pltpu.make_async_copy(mom, mom_out, out_sem.at[0])]
    stores[0].start()

    at = 0
    for i in range(4):
        total = None
        for a, b in terms(3):
            term = dot_t(lefts[a][i * 128 : (i + 1) * 128, :], lefts[b][i * 128 :, :])
            total = term if total is None else total + term
        for j in range(4 - i):
            for h in range(2):
                piece, rows = blocks_of(2 * at + h)
                partial[piece, rows, :] = total[h * 64 : (h + 1) * 64, j * 128 : (j + 1) * 128]
            at += 1

    def share(step, src, dst, sends, recvs):
        to = (grp, dev - x + lax.rem(x + step, 4))
        return remote(src, dst, sends.at[step - 1], recvs.at[step - 1], to)

    scatter = [
        share(step, partial.at[lax.rem(x + step, 4)], others.at[step - 1], rs_send, rs_recv)
        for step in (2, 1, 3)
    ]
    for copy in scatter:
        copy.start()
    for copy in scatter:
        copy.wait_recv()
    full[x] = (partial[x] + others[0]) + (others[1] + others[2])
    gather = [share(step, full.at[x], full.at[x], ag_send, ag_recv) for step in (2, 1, 3)]
    for copy in gather:
        copy.start()
    for copy in gather:
        copy.wait_recv()

    trace = None
    for at, (i, j) in enumerate(TILES):
        halves = [blocks_of(2 * at + h) for h in range(2)]
        tile = jnp.concatenate([full[piece, rows, :] for piece, rows in halves], axis=0)
        a_ref[i * 128 : (i + 1) * 128, j * 128 : (j + 1) * 128] = tile
        if i != j:
            a_ref[j * 128 : (j + 1) * 128, i * 128 : (i + 1) * 128] = tile.T
        else:
            row = lax.broadcasted_iota(jnp.int32, (128, 128), 0)
            col = lax.broadcasted_iota(jnp.int32, (128, 128), 1)
            diagonal = jnp.where(row == col, tile, 0.0)
            trace = diagonal if trace is None else trace + diagonal
    trace = jnp.sum(jnp.sum(trace, axis=0, keepdims=True), axis=1, keepdims=True)
    factor = 1.0 / (jnp.sqrt(trace) + norm_epsilon)
    for r in range(4):
        rows = slice(r * 128, (r + 1) * 128)
        x_ref[rows, :] = x_ref[rows, :] * factor
        a_ref[rows, :] = a_ref[rows, :] * (factor * factor)

    def load(slots, value_ref, count):
        for r in range(4):
            rows = slice(r * 128, (r + 1) * 128)
            value = value_ref[rows, :]
            for part_ref, part in zip(slots, split2(value) if count == 2 else split3(value)):
                part_ref[rows, :] = part

    def block(rows, cols, count):
        total = None
        for a, b in terms(count):
            term = dot(lefts[a][rows, :], rights[b][:, cols])
            total = term if total is None else total + term
        return total

    everywhere, high = slice(0, N), slice(HALF, N)

    def symmetric(dst, count, finish):
        for r in range(4):
            rows = slice(r * 128, (r + 1) * 128)
            cols = everywhere if r < 2 else high
            dst[rows, cols] = finish(block(rows, cols, count), rows, cols)
        for r in range(2):
            for s in range(2, 4):
                dst[s * 128 : (s + 1) * 128, r * 128 : (r + 1) * 128] = dst[
                    r * 128 : (r + 1) * 128, s * 128 : (s + 1) * 128
                ].T

    def iterate(count):
        load(lefts, a_ref, count)
        load(rights, a_ref, count)
        symmetric(b_ref, count, lambda v, r, c: second_coeff * a_ref[r, c] + third_coeff * v)
        load(lefts, b_ref, count)
        symmetric(t_ref, count, lambda v, r, c: first_coeff * a_ref[r, c] + v)
        load(rights, t_ref, count)
        symmetric(a_ref, count, lambda v, r, c: first_coeff * t_ref[r, c] + v)
        load(rights, x_ref, 2)
        for r in range(4):
            rows = slice(r * 128, (r + 1) * 128)
            x_ref[rows, :] = first_coeff * x_ref[rows, :] + block(rows, everywhere, 2)

    iterate(3)
    iterate(3)

    def middle(step, carry):
        iterate(2)
        return carry

    lax.fori_loop(2, ITERS - 1, middle, 0)

    def region(chunk, part):
        first = chunk // 2 * 128 + part * DEPTH
        return pl.ds(pl.multiple_of(first, DEPTH), DEPTH), slice(chunk % 2 * HALF, (chunk % 2 + 1) * HALF)

    def spread(chunk):
        part = held[chunk].at[pl.ds(0, 7)]
        return remote(part, part, s1_send.at[chunk], s1_recv.at[chunk], above)

    loads[2].wait()
    load(lefts, a_ref, 2)
    load(rights, a_ref, 2)
    x_high, x_low = x_parts = (p2, q2)
    for r in range(4):
        rows = slice(r * 128, (r + 1) * 128)
        value = x_ref[rows, :]
        for part_ref, part in zip(x_parts, split2(value)):
            part_ref[rows, :] = part
    for r in range(4):
        rows = slice(r * 128, (r + 1) * 128)
        mixed = second_coeff * a_ref[rows, :] + third_coeff * block(rows, everywhere, 2)
        mixed_high, mixed_low = split2(mixed)
        value = (
            dot(mixed_high, x_low[...]) + dot(mixed_low, x_high[...])
        ) + dot(mixed_high, x_high[...])
        step = (first_coeff * x_ref[rows, :] + value) * (0.2 * math.sqrt(max(N, 4 * N)))
        update[rows, :] = step
        weight = master[rows, :]
        weight = weight - learn_rate * (step + weight_decay * weight)
        master[rows, :] = weight
        rounded[rows, :] = weight.astype(BF16)
        for chunk in (2 * r, 2 * r + 1):
            for away in range(1, 8):
                to = lax.rem(mine + away, 8)
                remote(
                    rounded.at[region(chunk, to)], held[chunk].at[slot],
                    s1_send.at[chunk], s1_recv.at[chunk],
                    device(x, lax.div(to, 2), z, lax.rem(to, 2)),
                ).start()
            held[chunk][slot] = rounded[region(chunk, mine)]
    stores += [
        pltpu.make_async_copy(update, update_out, out_sem.at[1]),
        pltpu.make_async_copy(master, master_out, out_sem.at[2]),
    ]
    stores[1].start()
    stores[2].start()
    lookup.wait()

    def along(chunk, step, up):
        count = 8 if step < 4 else 4
        plane = lax.rem(z + 9 - step, 8) if up else lax.rem(z + step - 1, 8)
        first = plane * 8 + (0 if up or step < 4 else 4)
        part = held[chunk].at[pl.ds(first, count)]
        index = chunk * 4 + step - 1
        if up:
            return remote(part, part, up_send.at[index], up_recv.at[index], above)
        return remote(part, part, down_send.at[index], down_recv.at[index], below)

    def goal(chunk):
        first = x * N + chunk % 2 * HALF
        return rollout_out.at[region(chunk, mine)[0], pl.ds(pl.multiple_of(first, HALF), HALF)]

    def pick(chunk, index):
        chosen[chunk, index] = held[chunk][table[lax.rem(index, 2), 0, in_plane(index)[1]]]

    def deliver(chunk):
        target = goal(chunk)

        def give(step, carry):
            index = lax.rem(here + step, 32)
            pick(chunk, index)
            remote(
                chosen.at[chunk, index], target, s3_send.at[chunk], s3_recv, in_plane(index)
            ).start()
            return carry

        lax.fori_loop(1, 32, give, 0)
        pick(chunk, here)
        pltpu.make_async_copy(chosen.at[chunk, here], target, own_sem.at[chunk]).start()

    for chunk, step in SCHEDULE:
        if step == 1:
            spread(chunk).wait_recv()
        else:
            hop = step - 1 if step else 4
            along(chunk, hop, True).wait_recv()
            along(chunk, hop, False).wait_recv()
        if step:
            along(chunk, step, True).start()
            along(chunk, step, False).start()
        else:
            deliver(chunk)

    tell.wait_send()
    everything.wait_send()
    for copy in scatter + gather:
        copy.wait_send()
    for copy in stores:
        copy.wait()
    for chunk in range(CHUNKS):
        spread(chunk).wait_send()
        for step in range(1, 5):
            along(chunk, step, True).wait_send()
            along(chunk, step, False).wait_send()
        part = chosen.at[chunk, pl.ds(0, 31)]
        remote(part, part, s3_send.at[chunk], s3_recv, above).wait_send()
        pltpu.make_async_copy(chosen.at[chunk, here], goal(chunk), own_sem.at[chunk]).wait()
    arrived = rollout_out.at[pl.ds(0, 31 * 16), :]
    remote(arrived, arrived, s3_send.at[0], s3_recv, above).wait_recv()


def shards(gradient, momentum, master_weight, owned_matrix, rollout_matrix):
    smem, vmem, anywhere = (
        pl.BlockSpec(memory_space=space) for space in (pltpu.SMEM, pltpu.VMEM, pl.ANY)
    )
    dma = pltpu.SemaphoreType.DMA
    square = jax.ShapeDtypeStruct((N, N), F32)
    wide, half = pltpu.VMEM((N, N), F32), pltpu.VMEM((N, N), BF16)
    hops = dma((CHUNKS * 4,))
    box = pltpu.VMEM((DEVS, 16, HALF), BF16)
    moment, update, weight, rollout = pl.pallas_call(
        kernel,
        out_shape=(square, square, square, jax.ShapeDtypeStruct((N, 4 * N), BF16)),
        in_specs=[smem, vmem, anywhere, anywhere, anywhere],
        out_specs=(anywhere,) * 4,
        scratch_shapes=[pltpu.VMEM((QUADS, 8, 4 * N), BF16), wide, wide, wide]
        + [box, box]
        + [pltpu.VMEM((count, PIECE, 128), F32) for count in (4, 3, 4)]
        + [wide] * 4
        + [half] * 6
        + [
            half,
            pltpu.VMEM((CHUNKS, 32, DEPTH, HALF), BF16),
            pltpu.VMEM((2, 8, 128), jnp.int32),
            pltpu.VMEM((2, 8, 128), jnp.int32),
            pltpu.SMEM((2, 8, 128), jnp.int32),
        ]
        + [dma((3,)), dma((3,)), dma, dma, dma]
        + [dma, dma, dma((3,)), dma((3,)), dma((3,)), dma((3,))]
        + [dma((CHUNKS,)), dma((CHUNKS,)), hops, hops, hops, hops, dma((CHUNKS,)), dma, dma((CHUNKS,))]
        + [pltpu.VMEM((64, DEPTH, HALF), BF16)] * CHUNKS,
        compiler_params=pltpu.CompilerParams(
            collective_id=0, has_side_effects=True, vmem_limit_bytes=63 << 20
        ),
        name="muon",
    )(owned_matrix, rollout_matrix, gradient, momentum[0], master_weight[0])
    return (moment[None], update[None], weight[None], rollout[None])


def solution(mesh):
    everyone = P(("grp", "dev"), None, None)
    return jax.shard_map(
        shards,
        mesh=mesh,
        in_specs=(P("grp", "dev", None), everyone, everyone, P(), P("grp", None)),
        out_specs=(everyone,) * 4,
        check_vma=False,
    )
```

profile of v0, /device:TPU:1, one launch (start us, length us, event | category | flops | bytes accessed | tf_op | source)
XLA Modules:
  0.0 130.5 jit_solution(18101074930141692747)
XLA Ops:
  0.6 124.1 %muon.1 = (f32[512,512]{1,0:T(8,128)}, f32[512,512]{1,0:T(8,128)}, f32[512,512]{1,0:T(8,128)}, bf16[512,2048]{1,0:T(8,128)(2,1)}) custom-call(s32[4,16]{1,0:T(4,128)} %owned.1, s32[1,64]{1,0:T(1,128)} %wanted.1, bf16[16,8,2048]{2,1,0:T(8,128)(2,1)} %grad_in.1, f32[512,512]{1,0:T(8,128)} %bitcast.7, f32[512,512]{1,0:T(8,128)} %bitcast.8), custom_call_target="tpu_custom_call" | custom-call | tf_op jit(solution)/shard_map/muon/pallas_call | solution.py:413
  124.7 0.0 copy-start.2
  124.7 0.0 copy-start.1
  124.7 2.4 %copy.13 = f32[1,512,512]{2,1,0:T(8,128)} copy(f32[1,512,512]{2,1,0:T(8,128)} %bitcast.11) | data formatting | bytes 2097152
  127.1 0.0 copy-done.2
  127.1 0.0 copy-start
  127.1 1.0 copy.14
  128.1 0.0 copy-done.1
  128.1 1.0 copy.15
  129.1 0.1 copy-done
  129.2 1.3 %copy.16 = bf16[1,512,2048]{2,1,0:T(8,128)(2,1)} copy(bf16[1,512,2048]{2,1,0:T(8,128)(2,1)S(1)} %bitcast.6) | data formatting | bytes 4194304
Async XLA Ops:
  124.7 2.4 %copy-start.2 = (f32[512,512]{1,0:T(8,128)S(1)}, f32[512,512]{1,0:T(8,128)}, u32[]{:S(2)}) copy-start(f32[512,512]{1,0:T(8,128)} %get-tuple-element.9) | copy-start | bytes 3145732
  124.7 3.4 %copy-start.1 = (f32[512,512]{1,0:T(8,128)S(1)}, f32[512,512]{1,0:T(8,128)}, u32[]{:S(2)}) copy-start(f32[512,512]{1,0:T(8,128)} %get-tuple-element.10) | copy-start | bytes 3145732
  127.1 2.0 %copy-start = (bf16[512,2048]{1,0:T(8,128)(2,1)S(1)}, bf16[512,2048]{1,0:T(8,128)(2,1)}, u32[]{:S(2)}) copy-start(bf16[512,2048]{1,0:T(8,128)(2,1)} %get-tuple-element.11) | copy-start | bytes 6291460
where the time goes:
time: 131 us; the launch traced here: 130 us
  Pallas kernels  124 us (95%)
  local copies, waits for them, and re-layouts  5.75 us (4%)
    pallas_call x1, Pallas kernels, shards(): pl.pallas_call(kernel, out_shape=(square, square, square, jax.ShapeDtypeS...  124 us
    unnamed x10, local copies, waits for them, and re-layouts  5.75 us

commit v1 on v0

--- a/solution.py
+++ b/solution.py
@@ -56,11 +56,8 @@
 
 
 SCHEDULE = [
-    (int(step[0]), int(step[1]))
-    for step in (
-        "01 11 31 21 41 12 02 32 51 13 22 03 42 14 33 61 04 23 10 34 52 71 00 43 24 30 62 53 44 72"
-        " 20 63 54 40 73 64 50 74 60 70"
-    ).split(" ")
+    1, 11, 31, 21, 41, 12, 2, 32, 51, 13, 22, 3, 42, 14, 33, 61, 4, 23, 10, 34,
+    52, 71, 0, 43, 24, 30, 62, 53, 44, 72, 20, 63, 54, 40, 73, 64, 50, 74, 60, 70,
 ]
 
 
@@ -73,7 +70,8 @@
     mom_out, update_out, master_out, rollout_out,
     grad, mom, master, update,
     outbox, inbox, partial, others, full,
-    a_ref, b_ref, t_ref, x_ref, p0, p1, p2, q0, q1, q2,
+    a_ref, t_ref, x_ref,
+    a0, a1, a2, b0, b1, b2, t0, t1, t2, x0, x1, x2, x3,
     rounded, chosen, names, table_v, table,
     in_sem, out_sem, names_send, names_recv, table_sem,
     send_sem, recv_sem, rs_send, rs_recv, ag_send, ag_recv,
@@ -176,7 +174,8 @@
     )
     everything.wait_recv()
 
-    lefts, rights = (p0, p1, p2), (q0, q1, q2)
+    a_parts, b_parts, t_parts = (a0, a1, a2), (b0, b1, b2), (t0, t1, t2)
+    x_parts = ((x0, x1), (x2, x3))
     for r in range(4):
         got = inbox[pl.ds(r * 16, 16)].astype(F32)
         slab = jnp.concatenate(
@@ -187,8 +186,8 @@
         mom[rows, :] = moment
         nesterov = slab + momentum_decay * moment
         x_ref[rows, :] = nesterov
-        for left, part in zip(lefts, split3(nesterov)):
-            left[rows, :] = part
+        for part_ref, part in zip(b_parts, split3(nesterov)):
+            part_ref[rows, :] = part
     stores = [pltpu.make_async_copy(mom, mom_out, out_sem.at[0])]
     stores[0].start()
 
@@ -196,7 +195,7 @@
     for i in range(4):
         total = None
         for a, b in terms(3):
-            term = dot_t(lefts[a][i * 128 : (i + 1) * 128, :], lefts[b][i * 128 :, :])
+            term = dot_t(b_parts[a][i * 128 : (i + 1) * 128, :], b_parts[b][i * 128 :, :])
             total = term if total is None else total + term
         for j in range(4 - i):
             for h in range(2):
@@ -237,59 +236,61 @@
             trace = diagonal if trace is None else trace + diagonal
     trace = jnp.sum(jnp.sum(trace, axis=0, keepdims=True), axis=1, keepdims=True)
     factor = 1.0 / (jnp.sqrt(trace) + norm_epsilon)
+    everywhere, high = slice(0, N), slice(HALF, N)
+
+    def emit(value, rows, cols, whole, parts):
+        if whole is not None:
+            whole[rows, cols] = value
+        for part_ref, part in zip(parts, split2(value) if len(parts) == 2 else split3(value)):
+            part_ref[rows, cols] = part
+
     for r in range(4):
         rows = slice(r * 128, (r + 1) * 128)
-        x_ref[rows, :] = x_ref[rows, :] * factor
-        a_ref[rows, :] = a_ref[rows, :] * (factor * factor)
-
-    def load(slots, value_ref, count):
-        for r in range(4):
-            rows = slice(r * 128, (r + 1) * 128)
-            value = value_ref[rows, :]
-            for part_ref, part in zip(slots, split2(value) if count == 2 else split3(value)):
-                part_ref[rows, :] = part
-
-    def block(rows, cols, count):
+        emit(x_ref[rows, :] * factor, rows, everywhere, x_ref, x_parts[0])
+        emit(a_ref[rows, :] * (factor * factor), rows, everywhere, a_ref, a_parts)
+
+    def block(lefts, rights, rows, cols, count):
         total = None
         for a, b in terms(count):
             term = dot(lefts[a][rows, :], rights[b][:, cols])
             total = term if total is None else total + term
         return total
 
-    everywhere, high = slice(0, N), slice(HALF, N)
-
-    def symmetric(dst, count, finish):
+    def symmetric(lefts, rights, count, finish, whole, parts):
         for r in range(4):
             rows = slice(r * 128, (r + 1) * 128)
             cols = everywhere if r < 2 else high
-            dst[rows, cols] = finish(block(rows, cols, count), rows, cols)
-        for r in range(2):
-            for s in range(2, 4):
-                dst[s * 128 : (s + 1) * 128, r * 128 : (r + 1) * 128] = dst[
-                    r * 128 : (r + 1) * 128, s * 128 : (s + 1) * 128
-                ].T
-
-    def iterate(count):
-        load(lefts, a_ref, count)
-        load(rights, a_ref, count)
-        symmetric(b_ref, count, lambda v, r, c: second_coeff * a_ref[r, c] + third_coeff * v)
-        load(lefts, b_ref, count)
-        symmetric(t_ref, count, lambda v, r, c: first_coeff * a_ref[r, c] + v)
-        load(rights, t_ref, count)
-        symmetric(a_ref, count, lambda v, r, c: first_coeff * t_ref[r, c] + v)
-        load(rights, x_ref, 2)
+            value = finish(block(lefts, rights, rows, cols, count), rows, cols)
+            emit(value, rows, cols, whole, parts)
+            if r < 2:
+                for s in range(2, 4):
+                    mirror = slice(s * 128, (s + 1) * 128)
+                    emit(value[:, mirror].T, mirror, rows, whole, parts)
+
+    def iterate(step, count, following):
+        symmetric(
+            a_parts, a_parts, count,
+            lambda v, r, c: second_coeff * a_ref[r, c] + third_coeff * v,
+            None, b_parts[:count],
+        )
+        symmetric(
+            b_parts, a_parts, count,
+            lambda v, r, c: first_coeff * a_ref[r, c] + v,
+            t_ref, t_parts[:count],
+        )
+        symmetric(
+            b_parts, t_parts, count,
+            lambda v, r, c: first_coeff * t_ref[r, c] + v,
+            a_ref, a_parts[:following],
+        )
         for r in range(4):
             rows = slice(r * 128, (r + 1) * 128)
-            x_ref[rows, :] = first_coeff * x_ref[rows, :] + block(rows, everywhere, 2)
-
-    iterate(3)
-    iterate(3)
-
-    def middle(step, carry):
-        iterate(2)
-        return carry
-
-    lax.fori_loop(2, ITERS - 1, middle, 0)
+            value = block(b_parts, x_parts[step % 2], rows, everywhere, 2)
+            value = first_coeff * x_ref[rows, :] + value
+            emit(value, rows, everywhere, x_ref, x_parts[(step + 1) % 2])
+
+    for step, counts in enumerate(((3, 3), (3, 2), (2, 2), (2, 2))):
+        iterate(step, *counts)
 
     def region(chunk, part):
         first = chunk // 2 * 128 + part * DEPTH
@@ -300,21 +301,11 @@
         return remote(part, part, s1_send.at[chunk], s1_recv.at[chunk], above)
 
     loads[2].wait()
-    load(lefts, a_ref, 2)
-    load(rights, a_ref, 2)
-    x_high, x_low = x_parts = (p2, q2)
     for r in range(4):
         rows = slice(r * 128, (r + 1) * 128)
-        value = x_ref[rows, :]
-        for part_ref, part in zip(x_parts, split2(value)):
-            part_ref[rows, :] = part
-    for r in range(4):
-        rows = slice(r * 128, (r + 1) * 128)
-        mixed = second_coeff * a_ref[rows, :] + third_coeff * block(rows, everywhere, 2)
-        mixed_high, mixed_low = split2(mixed)
-        value = (
-            dot(mixed_high, x_low[...]) + dot(mixed_low, x_high[...])
-        ) + dot(mixed_high, x_high[...])
+        value = block(a_parts, a_parts, rows, everywhere, 2)
+        emit(second_coeff * a_ref[rows, :] + third_coeff * value, rows, everywhere, None, b_parts[:2])
+        value = block(b_parts, x_parts[0], rows, everywhere, 2)
         step = (first_coeff * x_ref[rows, :] + value) * (0.2 * math.sqrt(max(N, 4 * N)))
         update[rows, :] = step
         weight = master[rows, :]
@@ -370,7 +361,8 @@
         pick(chunk, here)
         pltpu.make_async_copy(chosen.at[chunk, here], target, own_sem.at[chunk]).start()
 
-    for chunk, step in SCHEDULE:
+    for code in SCHEDULE:
+        chunk, step = code // 10, code % 10
         if step == 1:
             spread(chunk).wait_recv()
         else:
@@ -418,8 +410,8 @@
         scratch_shapes=[pltpu.VMEM((QUADS, 8, 4 * N), BF16), wide, wide, wide]
         + [box, box]
         + [pltpu.VMEM((count, PIECE, 128), F32) for count in (4, 3, 4)]
-        + [wide] * 4
-        + [half] * 6
+        + [wide] * 3
+        + [half] * 13
         + [
             half,
             pltpu.VMEM((CHUNKS, 32, DEPTH, HALF), BF16),

time: 131 us -> 129 us (0.985)
    pallas_call x1, Pallas kernels: 124 us -> 123 us  [shards(): pl.pallas_call(kernel, out_shape=(square, square, square, jax.ShapeDtypeS...]
where the time goes in v1:
time: 129 us
  Pallas kernels  123 us (95%)
  local copies, waits for them, and re-layouts  5.75 us (4%)
    pallas_call x1, Pallas kernels, shards(): pl.pallas_call(kernel, out_shape=(square, square, square, jax.ShapeDtypeS...  123 us
    unnamed x10, local copies, waits for them, and re-layouts  5.75 us

profile of v1, /device:TPU:1, one launch (start us, length us, event | category | flops | bytes accessed | tf_op | source)
XLA Modules:
  0.0 128.9 jit_solution(13756290594244017068)
XLA Ops:
  0.6 122.5 %muon.1 = (f32[512,512]{1,0:T(8,128)}, f32[512,512]{1,0:T(8,128)}, f32[512,512]{1,0:T(8,128)}, bf16[512,2048]{1,0:T(8,128)(2,1)}) custom-call(s32[4,16]{1,0:T(4,128)} %owned.1, s32[1,64]{1,0:T(1,128)} %wanted.1, bf16[16,8,2048]{2,1,0:T(8,128)(2,1)} %grad_in.1, f32[512,512]{1,0:T(8,128)} %bitcast.7, f32[512,512]{1,0:T(8,128)} %bitcast.8), custom_call_target="tpu_custom_call" | custom-call | tf_op jit(solution)/shard_map/muon/pallas_call | solution.py:405
  123.2 0.0 copy-start.2
  123.2 0.0 copy-start.1
  123.2 2.4 %copy.13 = f32[1,512,512]{2,1,0:T(8,128)} copy(f32[1,512,512]{2,1,0:T(8,128)} %bitcast.11) | data formatting | bytes 2097152
  125.6 0.0 copy-done.2
  125.6 0.0 copy-start
  125.6 1.0 copy.14
  126.6 0.0 copy-done.1
  126.6 1.0 copy.15
  127.6 0.1 copy-done
  127.6 1.3 %copy.16 = bf16[1,512,2048]{2,1,0:T(8,128)(2,1)} copy(bf16[1,512,2048]{2,1,0:T(8,128)(2,1)S(1)} %bitcast.6) | data formatting | bytes 4194304
Async XLA Ops:
  123.2 2.4 %copy-start.2 = (f32[512,512]{1,0:T(8,128)S(1)}, f32[512,512]{1,0:T(8,128)}, u32[]{:S(2)}) copy-start(f32[512,512]{1,0:T(8,128)} %get-tuple-element.9) | copy-start | bytes 3145732
  123.2 3.4 %copy-start.1 = (f32[512,512]{1,0:T(8,128)S(1)}, f32[512,512]{1,0:T(8,128)}, u32[]{:S(2)}) copy-start(f32[512,512]{1,0:T(8,128)} %get-tuple-element.10) | copy-start | bytes 3145732
  125.6 2.0 %copy-start = (bf16[512,2048]{1,0:T(8,128)(2,1)S(1)}, bf16[512,2048]{1,0:T(8,128)(2,1)}, u32[]{:S(2)}) copy-start(bf16[512,2048]{1,0:T(8,128)(2,1)} %get-tuple-element.11) | copy-start | bytes 6291460

commit v2 on v1

--- a/solution.py
+++ b/solution.py
@@ -391,6 +391,44 @@
         pltpu.make_async_copy(chosen.at[chunk, here], goal(chunk), own_sem.at[chunk]).wait()
     arrived = rollout_out.at[pl.ds(0, 31 * 16), :]
     remote(arrived, arrived, s3_send.at[0], s3_recv, above).wait_recv()
+
+
+def publish_kernel(moment, update, weight, rollout, *refs):
+    outs, (buffer, load_sem, store_sem) = refs[:4], refs[4:]
+    loads, stores = [], []
+    for index in range(4):
+        rows = pl.ds(index * 128, 128)
+        loads.append(
+            pltpu.make_async_copy(rollout.at[rows, :], buffer.at[rows, :], load_sem.at[index])
+        )
+        loads[-1].start()
+    for index, (src, dst) in enumerate(zip((moment, update, weight), outs)):
+        stores.append(pltpu.make_async_copy(src, dst, store_sem.at[index]))
+        stores[-1].start()
+    for index in range(4):
+        rows = pl.ds(index * 128, 128)
+        loads[index].wait()
+        stores.append(
+            pltpu.make_async_copy(buffer.at[rows, :], outs[3].at[rows, :], store_sem.at[3 + index])
+        )
+        stores[-1].start()
+    for copy in stores:
+        copy.wait()
+
+
+def publish_call(moment, update, weight, rollout):
+    vmem, anywhere = pl.BlockSpec(memory_space=pltpu.VMEM), pl.BlockSpec(memory_space=pl.ANY)
+    dma = pltpu.SemaphoreType.DMA
+    results = (moment, update, weight, rollout)
+    return pl.pallas_call(
+        publish_kernel,
+        out_shape=tuple(jax.ShapeDtypeStruct(v.shape, v.dtype) for v in results),
+        in_specs=[vmem, vmem, vmem, anywhere],
+        out_specs=(anywhere,) * 4,
+        scratch_shapes=[pltpu.VMEM((N, 4 * N), BF16), dma((4,)), dma((7,))],
+        compiler_params=pltpu.CompilerParams(vmem_limit_bytes=50 << 20),
+        name="publish",
+    )(*results)
 
 
 def shards(gradient, momentum, master_weight, owned_matrix, rollout_matrix):
@@ -424,11 +462,12 @@
         + [dma((CHUNKS,)), dma((CHUNKS,)), hops, hops, hops, hops, dma((CHUNKS,)), dma, dma((CHUNKS,))]
         + [pltpu.VMEM((64, DEPTH, HALF), BF16)] * CHUNKS,
         compiler_params=pltpu.CompilerParams(
-            collective_id=0, has_side_effects=True, vmem_limit_bytes=63 << 20
+            collective_id=0, has_side_effects=True, vmem_limit_bytes=50 << 20
         ),
         name="muon",
     )(owned_matrix, rollout_matrix, gradient, momentum[0], master_weight[0])
-    return (moment[None], update[None], weight[None], rollout[None])
+    results = publish_call(moment, update, weight, rollout)
+    return tuple(result[None] for result in results)
 
 
 def solution(mesh):

time: 129 us -> 130 us (level)
  local copies, waits for them, and re-layouts: 5.75 us -> 2.37 us
  Pallas kernels: 123 us -> 126 us
    pallas_call x0 -> x1, Pallas kernels: none -> 3.75 us  [publish_call(): pl.pallas_call(publish_kernel, out_shape=tuple((jax.ShapeDtypeStruct(v.sh...]
    unnamed x10 -> x6, local copies, waits for them, and re-layouts: 5.75 us -> 2.37 us
where the time goes in v2:
time: 130 us
  Pallas kernels  126 us (97%)
  local copies, waits for them, and re-layouts  2.37 us (2%)
    pallas_call x1, Pallas kernels, shards(): pl.pallas_call(kernel, out_shape=(square, square, square, jax.ShapeDtypeS...  123 us
    pallas_call x1, Pallas kernels, publish_call(): pl.pallas_call(publish_kernel, out_shape=tuple((jax.ShapeDtypeStruct(v.sh...  3.75 us

profile of v2, /device:TPU:1, one launch (start us, length us, event | category | flops | bytes accessed | tf_op | source)
XLA Modules:
  0.0 129.6 jit_solution(15395456717100423550)
XLA Ops:
  0.6 0.0 copy-start
  0.6 1.0 copy-done
  1.7 0.0 copy-start.1
  1.7 0.7 copy-done.1
  2.4 0.0 copy-start.2
  2.4 0.7 copy-done.2
  3.0 122.6 %muon.1 = (f32[512,512]{1,0:T(8,128)S(1)}, f32[512,512]{1,0:T(8,128)S(1)}, f32[512,512]{1,0:T(8,128)S(1)}, bf16[512,2048]{1,0:T(8,128)(2,1)}) custom-call(s32[4,16]{1,0:T(4,128)S(1)} %copy-done.1, s32[1,64]{1,0:T(1,128)S(1)} %copy-done.2, bf16[16,8,2048]{2,1,0:T(8,128)(2,1)S(1)} %copy-done, f32[512,512]{1,0:T(8,128)} %bitcast.6, f32[512,512]{1,0:T(8,128)} %bitcast.7), custom_call_target="tpu_custom_call" | custom-call | tf_op jit(solution)/shard_map/muon/pallas_call | solution.py:443
  125.7 3.8 %publish.1 = (f32[512,512]{1,0:T(8,128)}, f32[512,512]{1,0:T(8,128)}, f32[512,512]{1,0:T(8,128)}, bf16[512,2048]{1,0:T(8,128)(2,1)}) custom-call(f32[512,512]{1,0:T(8,128)S(1)} %get-tuple-element.12.moment, f32[512,512]{1,0:T(8,128)S(1)} %get-tuple-element.13.update, f32[512,512]{1,0:T(8,128)S(1)} %get-tuple-element.14.weight, ...), custom_call_target="tpu_custom_call" | custom-call | tf_op jit(solution)/shard_map/publish/pallas_call | solution.py:423
Async XLA Ops:
  0.6 1.0 copy-start
  1.7 0.7 copy-start.1
  2.4 0.7 copy-start.2

commit v3 on v1

--- a/solution.py
+++ b/solution.py
@@ -27,7 +27,6 @@
 CHUNKS = 8
 DEPTH = 16
 TILES = [(i, j) for i in range(4) for j in range(i, 4)]
-PIECE = len(TILES) * 128 // 4
 
 
 def split2(value):
@@ -61,15 +60,22 @@
 ]
 
 
+FIRST = 8
+UNITS = (2, 3)
+
+
 def blocks_of(unit):
-    return unit // 5, slice(unit % 5 * 64, (unit % 5 + 1) * 64)
+    stage = 0 if unit < FIRST else 1
+    unit = unit - FIRST * stage
+    row = unit % UNITS[stage] * 64
+    return stage, unit // UNITS[stage], slice(row, row + 64)
 
 
 def kernel(
     owned, wanted, grad_in, mom_in, master_in,
     mom_out, update_out, master_out, rollout_out,
     grad, mom, master, update,
-    outbox, inbox, partial, others, full,
+    outbox, inbox, partial_a, partial_b, others_a, others_b, full_a, full_b,
     a_ref, t_ref, x_ref,
     a0, a1, a2, b0, b1, b2, t0, t1, t2, x0, x1, x2, x3,
     rounded, chosen, names, table_v, table,
@@ -191,6 +197,20 @@
     stores = [pltpu.make_async_copy(mom, mom_out, out_sem.at[0])]
     stores[0].start()
 
+    partial, others, full = (partial_a, partial_b), (others_a, others_b), (full_a, full_b)
+
+    def share(stage, step, src, dst, sends, recvs):
+        to, index = (grp, dev - x + lax.rem(x + step, 4)), stage * 3 + step - 1
+        return remote(src, dst, sends.at[index], recvs.at[index], to)
+
+    scatter, gather = [], []
+
+    def start_scatter(stage):
+        for step in (2, 1, 3):
+            src, dst = partial[stage].at[lax.rem(x + step, 4)], others[stage].at[step - 1]
+            scatter.append(share(stage, step, src, dst, rs_send, rs_recv))
+            scatter[-1].start()
+
     at = 0
     for i in range(4):
         total = None
@@ -199,33 +219,32 @@
             total = term if total is None else total + term
         for j in range(4 - i):
             for h in range(2):
-                piece, rows = blocks_of(2 * at + h)
-                partial[piece, rows, :] = total[h * 64 : (h + 1) * 64, j * 128 : (j + 1) * 128]
+                stage, piece, rows = blocks_of(2 * at + h)
+                partial[stage][piece, rows, :] = total[
+                    h * 64 : (h + 1) * 64, j * 128 : (j + 1) * 128
+                ]
             at += 1
-
-    def share(step, src, dst, sends, recvs):
-        to = (grp, dev - x + lax.rem(x + step, 4))
-        return remote(src, dst, sends.at[step - 1], recvs.at[step - 1], to)
-
-    scatter = [
-        share(step, partial.at[lax.rem(x + step, 4)], others.at[step - 1], rs_send, rs_recv)
-        for step in (2, 1, 3)
-    ]
-    for copy in scatter:
-        copy.start()
-    for copy in scatter:
-        copy.wait_recv()
-    full[x] = (partial[x] + others[0]) + (others[1] + others[2])
-    gather = [share(step, full.at[x], full.at[x], ag_send, ag_recv) for step in (2, 1, 3)]
-    for copy in gather:
-        copy.start()
+        if i == 0:
+            start_scatter(0)
+    start_scatter(1)
+    for stage in range(2):
+        for copy in scatter[stage * 3 : stage * 3 + 3]:
+            copy.wait_recv()
+        mine_part, theirs = partial[stage][x], others[stage]
+        full[stage][x] = (mine_part + theirs[0]) + (theirs[1] + theirs[2])
+        for step in (2, 1, 3):
+            block_ref = full[stage].at[x]
+            gather.append(share(stage, step, block_ref, block_ref, ag_send, ag_recv))
+            gather[-1].start()
     for copy in gather:
         copy.wait_recv()
 
     trace = None
     for at, (i, j) in enumerate(TILES):
         halves = [blocks_of(2 * at + h) for h in range(2)]
-        tile = jnp.concatenate([full[piece, rows, :] for piece, rows in halves], axis=0)
+        tile = jnp.concatenate(
+            [full[stage][piece, rows, :] for stage, piece, rows in halves], axis=0
+        )
         a_ref[i * 128 : (i + 1) * 128, j * 128 : (j + 1) * 128] = tile
         if i != j:
             a_ref[j * 128 : (j + 1) * 128, i * 128 : (i + 1) * 128] = tile.T
@@ -393,6 +412,38 @@
     remote(arrived, arrived, s3_send.at[0], s3_recv, above).wait_recv()
 
 
+def publish_kernel(*refs):
+    sources, targets, buffers, (load_sem, store_sem) = refs[:4], refs[4:8], refs[8:12], refs[12:]
+    loads = [
+        pltpu.make_async_copy(sources[index], buffers[index], load_sem.at[index])
+        for index in range(4)
+    ]
+    stores = [
+        pltpu.make_async_copy(buffers[index], targets[index], store_sem.at[index])
+        for index in range(4)
+    ]
+    for copy in loads:
+        copy.start()
+    for load, store in zip(loads, stores):
+        load.wait()
+        store.start()
+    for copy in stores:
+        copy.wait()
+
+
+def publish_call(*results):
+    anywhere, dma = pl.BlockSpec(memory_space=pl.ANY), pltpu.SemaphoreType.DMA
+    return pl.pallas_call(
+        publish_kernel,
+        out_shape=tuple(jax.ShapeDtypeStruct(v.shape, v.dtype) for v in results),
+        in_specs=[anywhere] * 4,
+        out_specs=(anywhere,) * 4,
+        scratch_shapes=[pltpu.VMEM(v.shape, v.dtype) for v in results] + [dma((4,)), dma((4,))],
+        compiler_params=pltpu.CompilerParams(vmem_limit_bytes=63 << 20),
+        name="publish",
+    )(*results)
+
+
 def shards(gradient, momentum, master_weight, owned_matrix, rollout_matrix):
     smem, vmem, anywhere = (
         pl.BlockSpec(memory_space=space) for space in (pltpu.SMEM, pltpu.VMEM, pl.ANY)
@@ -409,7 +460,7 @@
         out_specs=(anywhere,) * 4,
         scratch_shapes=[pltpu.VMEM((QUADS, 8, 4 * N), BF16), wide, wide, wide]
         + [box, box]
-        + [pltpu.VMEM((count, PIECE, 128), F32) for count in (4, 3, 4)]
+        + [pltpu.VMEM((count, units * 64, 128), F32) for count in (4, 3, 4) for units in UNITS]
         + [wide] * 3
         + [half] * 13
         + [
@@ -420,7 +471,7 @@
             pltpu.SMEM((2, 8, 128), jnp.int32),
         ]
         + [dma((3,)), dma((3,)), dma, dma, dma]
-        + [dma, dma, dma((3,)), dma((3,)), dma((3,)), dma((3,))]
+        + [dma, dma, dma((6,)), dma((6,)), dma((6,)), dma((6,))]
         + [dma((CHUNKS,)), dma((CHUNKS,)), hops, hops, hops, hops, dma((CHUNKS,)), dma, dma((CHUNKS,))]
         + [pltpu.VMEM((64, DEPTH, HALF), BF16)] * CHUNKS,
         compiler_params=pltpu.CompilerParams(
@@ -428,7 +479,8 @@
         ),
         name="muon",
     )(owned_matrix, rollout_matrix, gradient, momentum[0], master_weight[0])
-    return (moment[None], update[None], weight[None], rollout[None])
+    results = publish_call(moment, update, weight, rollout)
+    return tuple(result[None] for result in results)
 
 
 def solution(mesh):

time: 129 us -> 126 us (0.977)
  local copies, waits for them, and re-layouts: 5.75 us -> 0 us
  Pallas kernels: 123 us -> 125 us
    unnamed x10 -> x0, local copies, waits for them, and re-layouts: 5.75 us -> none
    pallas_call x0 -> x1, Pallas kernels: none -> 4.77 us  [publish_call(): pl.pallas_call(publish_kernel, out_shape=tuple((jax.ShapeDtypeStruct(v.sh...]
    pallas_call x1, Pallas kernels: 123 us -> 120 us  [shards(): pl.pallas_call(kernel, out_shape=(square, square, square, jax.ShapeDtypeS...]
where the time goes in v3:
time: 126 us; the launch traced here: 125 us
  Pallas kernels  125 us (99%)
    pallas_call x1, Pallas kernels, shards(): pl.pallas_call(kernel, out_shape=(square, square, square, jax.ShapeDtypeS...  120 us
    pallas_call x1, Pallas kernels, publish_call(): pl.pallas_call(publish_kernel, out_shape=tuple((jax.ShapeDtypeStruct(v.sh...  4.77 us

profile of v3, /device:TPU:1, one launch (start us, length us, event | category | flops | bytes accessed | tf_op | source)
XLA Modules:
  0.0 125.5 jit_solution(14134790648317226824)
XLA Ops:
  0.6 119.9 %muon.1 = (f32[512,512]{1,0:T(8,128)}, f32[512,512]{1,0:T(8,128)}, f32[512,512]{1,0:T(8,128)}, bf16[512,2048]{1,0:T(8,128)(2,1)}) custom-call(s32[4,16]{1,0:T(4,128)} %owned.1, s32[1,64]{1,0:T(1,128)} %wanted.1, bf16[16,8,2048]{2,1,0:T(8,128)(2,1)} %grad_in.1, f32[512,512]{1,0:T(8,128)} %bitcast.6, f32[512,512]{1,0:T(8,128)} %bitcast.7), custom_call_target="tpu_custom_call" | custom-call | tf_op jit(solution)/shard_map/muon/pallas_call | solution.py:456
  120.5 4.8 %publish.1 = (f32[512,512]{1,0:T(8,128)}, f32[512,512]{1,0:T(8,128)}, f32[512,512]{1,0:T(8,128)}, bf16[512,2048]{1,0:T(8,128)(2,1)}) custom-call(f32[512,512]{1,0:T(8,128)} %get-tuple-element.12.refs_0_, f32[512,512]{1,0:T(8,128)} %get-tuple-element.13.refs_1_, f32[512,512]{1,0:T(8,128)} %get-tuple-element.14.refs_2_, ...), custom_call_target="tpu_custom_call" | custom-call | tf_op jit(solution)/shard_map/publish/pallas_call | solution.py:436

commit v4 on v3

--- a/solution.py
+++ b/solution.py
@@ -129,8 +129,8 @@
         greet((z_lo * 2 + 1 - core, in_plane(2 * step)[1]))
         return carry
 
-    lax.fori_loop(1, DEVS, greet_group, 0)
-    lax.fori_loop(0, 16, greet_plane, 0)
+    lax.fori_loop(1, DEVS, greet_group, 0, unroll=9)
+    lax.fori_loop(0, 16, greet_plane, 0, unroll=8)
     greet(above)
     greet(below)
 
@@ -146,7 +146,7 @@
             outbox[q * 4 + c] = jnp.concatenate([left, right], axis=0).astype(BF16)
         return carry
 
-    lax.fori_loop(0, QUADS, fill, 0)
+    lax.fori_loop(0, QUADS, fill, 0, unroll=4)
     pl.semaphore_wait(barrier, DEVS - 1 + 18)
 
     def send(step, carry):
@@ -154,7 +154,7 @@
         remote(outbox.at[to], inbox.at[dev], send_sem, recv_sem, (grp, to)).start()
         return carry
 
-    lax.fori_loop(1, DEVS, send, 0)
+    lax.fori_loop(1, DEVS, send, 0, unroll=9)
     tell = remote(names.at[0], names.at[1], names_send, names_recv, twin)
     tell.start()
     inbox[dev] = outbox[dev]

time: 126 us -> 125 us (level)
  no operation moved by 1% of the time
where the time goes in v4:
time: 125 us
  Pallas kernels  125 us (100%)
    pallas_call x1, Pallas kernels, shards(): pl.pallas_call(kernel, out_shape=(square, square, square, jax.ShapeDtypeS...  120 us
    pallas_call x1, Pallas kernels, publish_call(): pl.pallas_call(publish_kernel, out_shape=tuple((jax.ShapeDtypeStruct(v.sh...  4.77 us

profile of v4, /device:TPU:1, one launch (start us, length us, event | category | flops | bytes accessed | tf_op | source)
XLA Modules:
  0.0 125.3 jit_solution(215762493645678040)
XLA Ops:
  0.6 119.7 %muon.1 = (f32[512,512]{1,0:T(8,128)}, f32[512,512]{1,0:T(8,128)}, f32[512,512]{1,0:T(8,128)}, bf16[512,2048]{1,0:T(8,128)(2,1)}) custom-call(s32[4,16]{1,0:T(4,128)} %owned.1, s32[1,64]{1,0:T(1,128)} %wanted.1, bf16[16,8,2048]{2,1,0:T(8,128)(2,1)} %grad_in.1, f32[512,512]{1,0:T(8,128)} %bitcast.6, f32[512,512]{1,0:T(8,128)} %bitcast.7), custom_call_target="tpu_custom_call" | custom-call | tf_op jit(solution)/shard_map/muon/pallas_call | solution.py:456
  120.4 4.8 %publish.1 = (f32[512,512]{1,0:T(8,128)}, f32[512,512]{1,0:T(8,128)}, f32[512,512]{1,0:T(8,128)}, bf16[512,2048]{1,0:T(8,128)(2,1)}) custom-call(f32[512,512]{1,0:T(8,128)} %get-tuple-element.12.refs_0_, f32[512,512]{1,0:T(8,128)} %get-tuple-element.13.refs_1_, f32[512,512]{1,0:T(8,128)} %get-tuple-element.14.refs_2_, ...), custom_call_target="tpu_custom_call" | custom-call | tf_op jit(solution)/shard_map/publish/pallas_call | solution.py:436
